TPU v7x, 512 devices: a whole 4x8x8 slice. The times are simulated.
512 devices in a mesh: dp: 16 (over z_hi, x, core), ctx: 32 (over y, z_lo).
Axes of the slice: x: 4, y: 8, z: 8 (z_hi: 2, z_lo: 4; z = z_hi * 4 + z_lo), core: 2. Of those that a mesh axis runs over, the one named last changes fastest.
Arguments:
- queries: bfloat16 [16, 16384, 512], P('dp', 'ctx'), may hold values from -36 to 36
- keys: bfloat16 [16, 16384, 512], P('dp', 'ctx'), may hold values from -36 to 36
- values: bfloat16 [16, 16384, 512], P('dp', 'ctx'), may hold values from -6 to 6
- grad_out: bfloat16 [16, 16384, 512], P('dp', 'ctx'), may hold values from -48 to 48
- gains: float32 [2, 512], replicated, may hold values from 0.1 to 1.9
Outputs:
- grad_queries: bfloat16 [16, 16384, 512], P('dp', 'ctx')
- grad_keys: bfloat16 [16, 16384, 512], P('dp', 'ctx')
- grad_values: bfloat16 [16, 16384, 512], P('dp', 'ctx')
- gain_grads: float32 [2, 512], P(None, 'dp')
All inputs are finite; a program needn't handle non-finite values.
Results may differ from a plain program's by a relative error of at most 0.0093.
Values may be sent and summed in bfloat16 or wider, within the bound.
A program may use at most 64 MiB of HBM per device.

v0:
```python
import math
import jax
import jax.numpy as jnp
from jax import lax
from jax.sharding import PartitionSpec as P

HEADS = 4
HD = 128
SPAN = 1
norm_eps = 1e-06


def from_behind(shard, axis, by):
    length = lax.axis_size(axis)
    pairs = [(i, i + by) for i in range(length) if 0 <= i + by < length]
    return lax.ppermute(shard, axis, pairs)


def unit_rows(inputs, heads):
    count = inputs.shape[0]
    wide = inputs.astype(jnp.float32).reshape(count, heads, -1)
    inverse = lax.rsqrt(jnp.mean(wide * wide, axis=2, keepdims=True) + norm_eps)
    return (wide * inverse, inverse)


def norm_backward(grad_norm, unit, inverse, gain):
    count, heads, head_dim = unit.shape
    grad_three = grad_norm.reshape(count, heads, head_dim)
    scaled = grad_three * gain
    mean_term = jnp.mean(scaled * unit, axis=2, keepdims=True)
    grad_in = inverse * (scaled - unit * mean_term)
    gain_grad = jnp.sum(grad_three * unit, axis=0).reshape(-1)
    return (grad_in.reshape(count, -1).astype(jnp.bfloat16), gain_grad)


def cross(left, right):
    return jnp.einsum("ad,cd->ac", left, right, preferred_element_type=jnp.float32)


def inner(left, right):
    return jnp.einsum("ac,ad->cd", left, right, preferred_element_type=jnp.float32)


def per_device(queries, keys, values, grad_out, gains):
    heads = HEADS
    head_dim = HD
    span = SPAN
    rows = queries.shape[1]
    reach = span * rows
    scale = 1.0 / math.sqrt(head_dim)
    place = lax.axis_index("ctx")
    q_unit, q_inv = unit_rows(queries[0], heads)
    k_unit, k_inv = unit_rows(keys[0], heads)
    q_gain = gains[0].reshape(heads, head_dim)
    k_gain = gains[1].reshape(heads, head_dim)
    q_norm = (q_unit * q_gain).reshape(rows, -1).astype(jnp.bfloat16)
    k_norm = (k_unit * k_gain).reshape(rows, -1).astype(jnp.bfloat16)
    upstream = grad_out[0]
    own = jnp.stack([k_norm, values[0]])
    tiles = [own]
    step = 1
    tiles.append(from_behind(own, "ctx", step))
    window = jnp.concatenate(tiles[::-1], axis=1)
    query_pos = lax.broadcasted_iota(jnp.int32, (rows, (span + 1) * rows), 0)
    key_pos = lax.broadcasted_iota(jnp.int32, (rows, (span + 1) * rows), 1)
    visible = (
        (key_pos > query_pos) & (key_pos <= query_pos + reach) & (key_pos >= (span - place) * rows)
    )
    first_key = 0
    dq_parts, dk_parts, dv_parts, lse_parts, delta_parts = ([], [], [], [], [])
    for head in range(heads):
        cols = slice(head * head_dim, (head + 1) * head_dim)
        q_head = q_norm[:, cols]
        k_head = window[0, :, cols]
        v_head = window[1, :, cols]
        g_head = upstream[:, cols]
        scores = cross(q_head, k_head) * scale
        total = jnp.sum(jnp.where(visible, jnp.exp(scores), 0.0), axis=1, keepdims=True)
        log_total = jnp.log(total)
        probs = jnp.where(visible, jnp.exp(scores - log_total), 0.0)
        probs_low = probs.astype(jnp.bfloat16)
        attended = jnp.dot(probs_low, v_head, preferred_element_type=jnp.float32)
        delta = jnp.sum(g_head.astype(jnp.float32) * attended, axis=1, keepdims=True)
        grad_scores = (probs * (cross(g_head, v_head) - delta)).astype(jnp.bfloat16)
        dq_parts.append(jnp.dot(grad_scores, k_head, preferred_element_type=jnp.float32) * scale)
        dk_parts.append(inner(grad_scores, q_head) * scale)
        dv_parts.append(inner(probs_low, g_head))
        lse_parts.append(log_total[:, 0])
        delta_parts.append(delta[:, 0])
    grad_qn = jnp.concatenate(dq_parts, axis=1)
    key_grads = jnp.stack([jnp.concatenate(dk_parts, axis=1), jnp.concatenate(dv_parts, axis=1)])
    local = key_grads[:, span * rows :]
    step = 1
    term = key_grads[:, (span - step) * rows : (span - step + 1) * rows]
    local = local + from_behind(term, "ctx", -step)
    grad_queries, q_gain_grad = norm_backward(grad_qn, q_unit, q_inv, q_gain)
    grad_keys, k_gain_grad = norm_backward(local[0], k_unit, k_inv, k_gain)
    grad_values = local[1].astype(jnp.bfloat16)
    gain_terms = jnp.stack([q_gain_grad, k_gain_grad])
    gain_total = lax.psum(gain_terms, "ctx")
    gain_share = lax.psum_scatter(gain_total, "dp", scatter_dimension=1, tiled=True)
    return (grad_queries[None], grad_keys[None], grad_values[None], gain_share)


def solution(mesh):
    placed = (
        P("dp", "ctx", None),
        P("dp", "ctx", None),
        P("dp", "ctx", None),
        P("dp", "ctx", None),
        P(),
    )
    return jax.shard_map(
        per_device,
        mesh=mesh,
        in_specs=placed,
        out_specs=(P("dp", "ctx", None), P("dp", "ctx", None), P("dp", "ctx", None), P(None, "dp")),
        check_vma=False,
    )
```

profile of v0, /device:TPU:2, one launch (start us, length us, event | category | flops | bytes accessed | tf_op | source)
XLA Modules:
  0.0 287.6 jit_solution(17089914442977109020)
XLA Ops:
  7.2 0.8 fusion.47
  8.0 1.3 copy.21
  9.2 1.3 copy.22
  10.5 1.2 multiply_reduce_fusion.3
  11.8 1.1 pad_maximum_fusion.1
  13.0 5.3 %collective-permute-start = (bf16[2,512,512]{1,2,0:T(8,128)(2,1)}, bf16[2,512,512]{1,2,0:T(8,128)(2,1)}, u32[]{:S(2)}, u32[]{:S(2)}) collective-permute-start(bf16[2,512,512]{1,2,0:T(8,128)(2,1)} %pad_maximum_fusion.1), channel_id=1, source_target_pairs={{0,1},{1,2},{2,3},{3,4},{4,5},{5,6},{6,7},{7,8},{8,9},{9,10},{10,1... | collective-permute-start | bytes 3145736 | tf_op jit(solution)/shard_map/ppermute | solution.py:16
  18.4 1.3 copy.23
  20.1 19.8 %collective-permute-done = bf16[2,512,512]{1,2,0:T(8,128)(2,1)} collective-permute-done((bf16[2,512,512]{1,2,0:T(8,128)(2,1)}, bf16[2,512,512]{1,2,0:T(8,128)(2,1)}, u32[]{:S(2)}, u32[]{:S(2)}) %collective-permute-start) | collective-permute-done | bytes 1048608 | tf_op jit(solution)/shard_map/ppermute | solution.py:16
  40.0 1.5 maximum_maximum_fusion
  41.5 0.5 fusion.26
  42.0 0.5 fusion.25
  42.4 0.5 fusion.24
  42.9 2.0 select_reduce_fusion.3
  44.9 2.4 fusion.8
  47.4 0.5 fusion.12
  47.9 0.3 fusion.44
  48.2 0.5 fusion.14
  48.7 0.3 fusion.38
  49.0 0.5 fusion.13
  49.5 0.3 fusion.41
  49.8 0.5 fusion.15
  50.3 0.3 fusion.35
  50.6 1.0 fusion.5
  51.6 1.0 fusion.3
  52.7 1.0 fusion.4
  53.7 1.0 fusion.2
  54.7 0.3 convolution_multiply_fusion
  55.0 0.3 convolution_multiply_fusion.2
  55.3 0.3 convolution_multiply_fusion.3
  55.6 0.3 convolution_multiply_fusion.1
  55.9 0.6 maximum_bitcast_fusion
  56.8 1.5 collective-permute-start.1
  58.3 0.5 convolution_multiply_fusion.4
  58.8 0.5 convolution_multiply_fusion.8
  59.3 0.5 convolution_multiply_fusion.6
  59.8 0.5 convolution_multiply_fusion.10
  60.6 0.4 fusion.19
  61.0 44.9 %collective-permute-done.1 = f32[2,512,512]{1,2,0:T(8,128)S(1)} collective-permute-done((f32[2,512,512]{1,2,0:T(8,128)S(1)}, f32[2,512,512]{1,2,0:T(8,128)S(1)}, u32[]{:S(2)}, u32[]{:S(2)}) %collective-permute-start.1) | collective-permute-done | bytes 2097184 | tf_op jit(solution)/shard_map/ppermute | solution.py:16
  105.9 0.5 fusion.1
  106.5 1.1 copy-done
  107.9 1.1 multiply_reduce_fusion
  109.0 0.9 copy.35
  109.9 1.0 copy.28
  111.0 1.0 copy.30
  112.0 1.0 copy.29
  113.0 88.8 %reduce-scatter.4.cloned.1.call-done = f32[32,2]{1,0:T(8,128)} async-done(((f32[512,2]{1,0:T(8,128)}), f32[32,2]{1,0:T(8,128)}) %reduce-scatter.4.cloned.1.call-update) | async-done | bytes 272
  201.8 0.8 copy.36
  202.5 78.3 %psum.8 = f32[2,32]{1,0:T(2,128)} all-reduce(f32[2,32]{1,0:T(2,128)S(1)} %copy.36), channel_id=1, replica_groups=mesh['dp'=16,'ctx'=32] {'ctx'}, use_global_device_ids=true, to_apply=%region_14.15 | all-reduce | flops 64 | bytes 512 | tf_op jit(solution)/shard_map/psum | solution.py:100
  (28 shorter events, 1.8 us)
Async XLA Ops:
  7.2 194.6 %reduce-scatter.4.cloned.1.call-start = ((), (), s32[]{:S(2)}) async-start(), calls=%async_computation.1 | async-start | bytes 278528
  10.5 7.7 %copy-start.2 = (bf16[1,512,512]{2,1,0:T(8,128)(2,1)S(1)}, bf16[1,512,512]{2,1,0:T(8,128)(2,1)}, u32[]{:S(2)}) copy-start(bf16[1,512,512]{2,1,0:T(8,128)(2,1)} %param.5) | copy-start | bytes 1572868
  13.0 27.0 %collective-permute-start = (bf16[2,512,512]{1,2,0:T(8,128)(2,1)}, bf16[2,512,512]{1,2,0:T(8,128)(2,1)}, u32[]{:S(2)}, u32[]{:S(2)}) collective-permute-start(bf16[2,512,512]{1,2,0:T(8,128)(2,1)} %pad_maximum_fusion.1), channel_id=1, source_target_pairs={{0,1},{1,2},{2,3},{3,4},{4,5},{5,6},{6,7},{7,8},{8,9},{9,10},{10,1... | collective-permute-start | bytes 3145736 | tf_op jit(solution)/shard_map/ppermute | solution.py:16
  56.8 49.1 %collective-permute-start.1 = (f32[2,512,512]{1,2,0:T(8,128)S(1)}, f32[2,512,512]{1,2,0:T(8,128)S(1)}, u32[]{:S(2)}, u32[]{:S(2)}) collective-permute-start(f32[2,512,512]{1,2,0:T(8,128)S(1)} %pad_maximum_fusion), channel_id=1, source_target_pairs={{1,0},{2,1},{3,2},{4,3},{5,4},{6,5},{7,6},{8,7},{9,8},{10,9},{11,1... | collective-permute-start | bytes 6291464 | tf_op jit(solution)/shard_map/ppermute | solution.py:16
  106.4 1.2 copy-start
  110.9 1.1 copy-start.1
Sparse Core Ops, SparseCore 0:
  110.0 91.6 reduce-scatter.3
where the time goes:
time: 288 us
  waiting for transfers between devices  154 us (53%)
  blocking collectives  78.3 us (27%)
  between operations  14.4 us (5%)
  matrix products  13.8 us (5%)
  local copies, waits for them, and re-layouts  10.7 us (4%)
  other arithmetic  10.2 us (4%)
  starting transfers between devices  6.81 us (2%)
    unnamed x2, waiting for transfers between devices  88.8 us
    psum x1, blocking collectives, per_device(): gain_total = lax.psum(gain_terms, 'ctx')  78.3 us
    ppermute x2, waiting for transfers between devices, from_behind(): return lax.ppermute(shard, axis, pairs)  64.8 us
    unnamed x15, local copies, waits for them, and re-layouts  9.78 us
    dot_general x8, matrix products, cross(): jnp.einsum('ad,cd->ac', left, right, preferred_element_type=jnp.float32)  7.34 us
    ppermute x2, starting transfers between devices, from_behind(): return lax.ppermute(shard, axis, pairs)  6.77 us
  transfers between devices with their start and end apart: 3, of which 3 were waited for; matrix products, arithmetic and copies ran while one was open for 3% of the time, Pallas kernels for 0%

commit v1 on v0

--- a/solution.py
+++ b/solution.py
@@ -97,7 +97,7 @@
     grad_keys, k_gain_grad = norm_backward(local[0], k_unit, k_inv, k_gain)
     grad_values = local[1].astype(jnp.bfloat16)
     gain_terms = jnp.stack([q_gain_grad, k_gain_grad])
-    gain_total = lax.psum(gain_terms, "ctx")
+    gain_total = jnp.sum(lax.all_gather(gain_terms, "ctx"), axis=0)
     gain_share = lax.psum_scatter(gain_total, "dp", scatter_dimension=1, tiled=True)
     return (grad_queries[None], grad_keys[None], grad_values[None], gain_share)
 

time: 288 us -> 288 us (level)
  the two profiles are of different devices: /device:TPU:2 before, /device:TPU:8 now
where the time goes in v1:
time: 288 us
  waiting for transfers between devices  162 us (56%)
  blocking collectives  68.1 us (24%)
  between operations  14.4 us (5%)
  matrix products  13.8 us (5%)
  local copies, waits for them, and re-layouts  11.3 us (4%)
  other arithmetic  10.3 us (4%)
  starting transfers between devices  8.17 us (3%)
    unnamed x2, waiting for transfers between devices  94.7 us
    all_gather x1, blocking collectives, per_device(): gain_total = jnp.sum(lax.all_gather(gain_terms, 'ctx'), axis=0)  68.1 us
    ppermute x2, waiting for transfers between devices, from_behind(): return lax.ppermute(shard, axis, pairs)  67.2 us
    unnamed x15, local copies, waits for them, and re-layouts  10.3 us
    ppermute x2, starting transfers between devices, from_behind(): return lax.ppermute(shard, axis, pairs)  8.14 us
    dot_general x8, matrix products, cross(): jnp.einsum('ad,cd->ac', left, right, preferred_element_type=jnp.float32)  7.34 us
  transfers between devices with their start and end apart: 3, of which 3 were waited for; matrix products, arithmetic and copies ran while one was open for 3% of the time, Pallas kernels for 0%

profile of v1, /device:TPU:8, one launch (start us, length us, event | category | flops | bytes accessed | tf_op | source)
XLA Modules:
  0.0 287.8 jit_solution(108849875713759106)
XLA Ops:
  7.2 0.8 fusion.47
  8.0 1.3 copy.21
  9.2 1.3 copy.22
  10.5 1.2 multiply_reduce_fusion.3
  11.8 1.1 pad_maximum_fusion.1
  13.0 4.3 %collective-permute-start = (bf16[2,512,512]{1,2,0:T(8,128)(2,1)}, bf16[2,512,512]{1,2,0:T(8,128)(2,1)}, u32[]{:S(2)}, u32[]{:S(2)}) collective-permute-start(bf16[2,512,512]{1,2,0:T(8,128)(2,1)} %pad_maximum_fusion.1), channel_id=1, source_target_pairs={{0,1},{1,2},{2,3},{3,4},{4,5},{5,6},{6,7},{7,8},{8,9},{9,10},{10,1... | collective-permute-start | bytes 3145736 | tf_op jit(solution)/shard_map/ppermute | solution.py:16
  17.5 1.3 copy.23
  19.1 25.1 %collective-permute-done = bf16[2,512,512]{1,2,0:T(8,128)(2,1)} collective-permute-done((bf16[2,512,512]{1,2,0:T(8,128)(2,1)}, bf16[2,512,512]{1,2,0:T(8,128)(2,1)}, u32[]{:S(2)}, u32[]{:S(2)}) %collective-permute-start) | collective-permute-done | bytes 1048608 | tf_op jit(solution)/shard_map/ppermute | solution.py:16
  44.2 1.5 maximum_maximum_fusion
  45.7 0.5 fusion.26
  46.2 0.5 fusion.25
  46.7 0.5 fusion.24
  47.1 2.0 select_reduce_fusion.3
  49.2 2.4 fusion.8
  51.6 0.5 fusion.12
  52.1 0.3 fusion.44
  52.4 0.5 fusion.14
  52.9 0.3 fusion.38
  53.2 0.5 fusion.13
  53.8 0.3 fusion.41
  54.1 0.5 fusion.15
  54.6 0.3 fusion.35
  54.9 1.0 fusion.5
  55.9 1.0 fusion.3
  56.9 1.0 fusion.4
  57.9 1.0 fusion.2
  58.9 0.3 convolution_multiply_fusion
  59.2 0.3 convolution_multiply_fusion.2
  59.5 0.3 convolution_multiply_fusion.3
  59.9 0.3 convolution_multiply_fusion.1
  60.2 0.6 maximum_bitcast_fusion
  61.0 3.9 %collective-permute-start.1 = (f32[2,512,512]{1,2,0:T(8,128)S(1)}, f32[2,512,512]{1,2,0:T(8,128)S(1)}, u32[]{:S(2)}, u32[]{:S(2)}) collective-permute-start(f32[2,512,512]{1,2,0:T(8,128)S(1)} %pad_maximum_fusion), channel_id=1, source_target_pairs={{1,0},{2,1},{3,2},{4,3},{5,4},{6,5},{7,6},{8,7},{9,8},{10,9},{11,1... | collective-permute-start | bytes 6291464 | tf_op jit(solution)/shard_map/ppermute | solution.py:16
  64.9 0.5 convolution_multiply_fusion.4
  65.4 0.5 convolution_multiply_fusion.8
  65.9 0.5 convolution_multiply_fusion.6
  66.4 0.5 convolution_multiply_fusion.10
  67.2 0.4 fusion.19
  67.6 42.1 %collective-permute-done.1 = f32[2,512,512]{1,2,0:T(8,128)S(1)} collective-permute-done((f32[2,512,512]{1,2,0:T(8,128)S(1)}, f32[2,512,512]{1,2,0:T(8,128)S(1)}, u32[]{:S(2)}, u32[]{:S(2)}) %collective-permute-start.1) | collective-permute-done | bytes 2097184 | tf_op jit(solution)/shard_map/ppermute | solution.py:16
  109.7 0.5 fusion.1
  110.3 1.1 copy-done
  111.7 1.1 multiply_reduce_fusion
  112.9 68.1 %all-gather.1 = f32[32,2,512]{2,1,0:T(2,128)S(1)} all-gather(f32[1,2,512]{2,1,0:T(2,128)S(1)} %maximum_bitcast_fusion.2), channel_id=2, replica_groups=mesh['dp'=16,'ctx'=32] {'ctx'}, dimensions={0}, use_global_device_ids=true | all-gather | bytes 135168 | tf_op jit(solution)/shard_map/all_gather | solution.py:100
  181.0 0.9 copy.35
  181.9 1.0 copy.28
  182.9 1.0 copy.30
  183.9 1.0 copy.29
  184.9 94.7 %reduce-scatter.4.cloned.1.call-done = f32[32,2]{1,0:T(8,128)} async-done(((f32[512,2]{1,0:T(8,128)}), f32[32,2]{1,0:T(8,128)}) %reduce-scatter.4.cloned.1.call-update) | async-done | bytes 272
  279.6 1.4 copy.36
  (29 shorter events, 1.9 us)
Async XLA Ops:
  7.2 272.5 %reduce-scatter.4.cloned.1.call-start = ((), (), s32[]{:S(2)}) async-start(), calls=%async_computation.1 | async-start | bytes 278528
  10.5 6.8 %copy-start.2 = (bf16[1,512,512]{2,1,0:T(8,128)(2,1)S(1)}, bf16[1,512,512]{2,1,0:T(8,128)(2,1)}, u32[]{:S(2)}) copy-start(bf16[1,512,512]{2,1,0:T(8,128)(2,1)} %param.5) | copy-start | bytes 1572868
  13.0 31.2 %collective-permute-start = (bf16[2,512,512]{1,2,0:T(8,128)(2,1)}, bf16[2,512,512]{1,2,0:T(8,128)(2,1)}, u32[]{:S(2)}, u32[]{:S(2)}) collective-permute-start(bf16[2,512,512]{1,2,0:T(8,128)(2,1)} %pad_maximum_fusion.1), channel_id=1, source_target_pairs={{0,1},{1,2},{2,3},{3,4},{4,5},{5,6},{6,7},{7,8},{8,9},{9,10},{10,1... | collective-permute-start | bytes 3145736 | tf_op jit(solution)/shard_map/ppermute | solution.py:16
  61.0 48.7 %collective-permute-start.1 = (f32[2,512,512]{1,2,0:T(8,128)S(1)}, f32[2,512,512]{1,2,0:T(8,128)S(1)}, u32[]{:S(2)}, u32[]{:S(2)}) collective-permute-start(f32[2,512,512]{1,2,0:T(8,128)S(1)} %pad_maximum_fusion), channel_id=1, source_target_pairs={{1,0},{2,1},{3,2},{4,3},{5,4},{6,5},{7,6},{8,7},{9,8},{10,9},{11,1... | collective-permute-start | bytes 6291464 | tf_op jit(solution)/shard_map/ppermute | solution.py:16
  110.2 1.2 copy-start
  182.9 1.1 copy-start.1
Sparse Core Ops, SparseCore 0:
  182.0 97.6 reduce-scatter.3
